TPU v7x, 32 devices: a whole 2x2x4 slice. The times are simulated.
32 devices in a mesh: gx: 8 (over z, x), gy: 4 (over y, core).
Axes of the slice: x: 2, y: 2, z: 4, core: 2. Of those that a mesh axis runs over, the one named last changes fastest.
Arguments:
- geometry: float32 [8, 131072], P(None, ('gx', 'gy')), may hold values from -1 to 9, as said below
- panel: bfloat16 [131072, 128], P(('gx', 'gy')), may hold values from -6 to 6
- pair_first: int32 [2048], P(('gx', 'gy')), may hold values from 0 to 7
- pair_second: int32 [2048], P(('gx', 'gy')), may hold values from 0 to 71, as said below
- pair_count: int32 [32], P(('gx', 'gy')), may hold values from 1 to 64, as said below
Outputs:
- near_product: float32 [131072, 128], P(('gx', 'gy'))
Inputs may be any that keep to these rules, and one draw needn't show every extreme that they name: `geometry`: rows are x, y, z, the unit direction's three components, the length and the radius; lengths lie in 0.25 to 4, radii in 0.005 to 0.02, and a filament of the device at (ix, iy) has x in ix - 0.5 to ix + 1.5 and y in iy - 0.5 to iy + 1.5. `pair_second`: the device named by every slot lies inside the grid of devices; slots at or beyond a device's count hold arbitrary entries of the same form; pairs may repeat. `pair_count`: some device uses all 64 slots.
All inputs are finite; a program needn't handle non-finite values.
Results may differ from a plain program's by a relative error of at most 0.0032.
Values may be sent and summed in bfloat16 or wider, within the bound.
A program may use at most 128 MiB of HBM per device.

v0:
```python
import functools

import jax
import jax.numpy as jnp
from jax import lax
from jax.experimental import pallas as pl
from jax.experimental.pallas import tpu as pltpu
from jax.sharding import PartitionSpec as P

BLOCK = 512
CHUNKS = 4
PART = 512
GRID = 16.0
MESH = pl.DeviceIdType.MESH
VMEM_LIMIT = 56 * 1024 * 1024


def split(value):
    high = value.astype(jnp.bfloat16).astype(jnp.float32)
    return high, value - high


def features(geo, gx, gy, own):
    kind = lax.broadcasted_iota(jnp.int32, geo.shape, 0)
    place = kind < 3
    centre = jnp.where(kind == 0, gx.astype(jnp.float32) + 0.5, jnp.where(kind == 1, gy.astype(jnp.float32) + 0.5, 4.0))
    local = geo - centre
    coarse = jnp.where(place, jnp.floor(local * GRID + 0.5) * (1.0 / GRID), 0.0)
    fine = jnp.where(place, local - coarse, 0.0)
    radius = jnp.where(kind == 7, geo, 0.0)
    fine_high, rest = split(fine)
    fine_mid, fine_low = split(rest)
    both_high, both_low = split(fine + radius)
    norm = jnp.broadcast_to(jnp.sum(coarse * coarse, axis=0, keepdims=True), geo.shape)
    extra = jnp.broadcast_to(jnp.sum((2.0 * coarse + fine) * fine + radius * radius, axis=0, keepdims=True), geo.shape)
    norm_high, norm_low = split(norm)
    extra_high, rest = split(extra)
    extra_mid, extra_low = split(rest)
    direction = jnp.where((kind >= 3) & (kind <= 5), geo * geo[6:7, :], 0.0)
    blank = jnp.zeros_like(geo)
    if own:
        high, low = split(direction * BLOCK ** (-0.5))
        norms = jnp.where(kind == 0, norm_high, jnp.where(kind == 1, norm_low, jnp.where(kind <= 3, 1.0, 0.0)))
        extras = jnp.where(kind == 0, extra_high, jnp.where(kind == 1, extra_mid, jnp.where(
            kind == 2, extra_low, jnp.where(kind <= 5, 1.0, 0.0))))
        groups = [high, high, low, blank, coarse, norms, both_high, both_high, both_low,
                  coarse, coarse, coarse, fine_high, fine_mid, fine_low, extras]
    else:
        high, low = split(direction)
        sign = jnp.where(place, -2.0, 2.0)
        norms = jnp.where(kind <= 1, 1.0, jnp.where(kind == 2, norm_high, jnp.where(kind == 3, norm_low, 0.0)))
        extras = jnp.where(kind <= 2, 1.0, jnp.where(kind == 3, extra_high, jnp.where(
            kind == 4, extra_mid, jnp.where(kind == 5, extra_low, 0.0))))
        double = -2.0 * coarse
        groups = [high, low, high, blank, double, norms, sign * both_high, sign * both_low, sign * both_high,
                  -2.0 * fine_high, -2.0 * fine_mid, -2.0 * fine_low, double, double, double, extras]
    return jnp.concatenate(groups, axis=0)


def prepare_own(block, geo_ref, gx, gy, own_along, own_coarse, own_fine):
    lanes = pl.ds(pl.multiple_of(block * BLOCK, BLOCK), BLOCK)
    turned = features(geo_ref[:, lanes], gx, gy, True).T.astype(jnp.bfloat16)
    own_along[block] = turned[:, 0:32]
    own_coarse[block] = turned[:, 32:48]
    own_fine[block] = turned[:, 48:128]


def align_part(c, a, b, own, feats, work):
    own_along, own_coarse, own_fine = own
    aligned, square = work
    here = pl.ds(c * PART, PART)
    aligned[here, :] = jnp.dot(own_along[a, here, :], feats[b, 0:32, :], preferred_element_type=jnp.float32)
    square[here, :] = jnp.dot(
        own_coarse[a, here, :], feats[b, 32:48, :], preferred_element_type=jnp.float32
    ) + jnp.dot(own_fine[a, here, :], feats[b, 48:128, :], preferred_element_type=jnp.float32)


def tile_part(c, work, tile):
    aligned, square = work
    for r in range(c * PART, (c + 1) * PART, 16):
        here = pl.ds(r, 16)
        tile[here, :] = (aligned[here, :] * lax.rsqrt(square[here, :])).astype(jnp.bfloat16)


def halo_kernel(nx, ny, table_ref, list_ref, geo_ref, pan_ref, lists, pans, tiles, feats,
                geos, own_along, own_coarse, own_fine, aligned0, aligned1, square0, square1, tile0, tile1, tile2, tile3,
                x_send, x_recv, z_send, z_recv, y_send, y_recv, out_sems):
    own = own_along, own_coarse, own_fine
    work0, work1 = (aligned0, square0), (aligned1, square1)
    gx = lax.axis_index("gx")
    gy = lax.axis_index("gy")
    fil = pan_ref.shape[0]
    step = fil // CHUNKS
    items = CHUNKS + 2
    blocks = fil // BLOCK
    rounds = tiles.shape[0] // 4
    odd = lax.rem(gx, 2)
    partner = gx + 1 - 2 * odd
    relay_to = gx + 2 - 4 * odd
    relay_from = gx - 2 + 4 * odd
    has_to = (relay_to >= 0) & (relay_to < nx)
    has_from = (relay_from >= 0) & (relay_from < nx)
    has_up = gy + 1 < ny
    has_down = gy >= 1
    near_row = 2 - 2 * odd
    far_row = 2 * odd

    def part(k, own, row, col):
        if k == 0:
            return list_ref if own else lists.at[row * 3 + col]
        if k == 1:
            return geo_ref if own else geos.at[row * 3 + col]
        rows = pl.ds((k - 2) * step, step)
        return pan_ref.at[rows] if own else pans.at[row * 3 + col, rows]

    def x_copy(k):
        return pltpu.make_async_remote_copy(
            src_ref=part(k, True, 1, 1), dst_ref=part(k, False, far_row, 1),
            send_sem=x_send.at[k], recv_sem=x_recv.at[k],
            device_id=(partner, gy), device_id_type=MESH)

    def x_arrival(k):
        return pltpu.make_async_remote_copy(
            src_ref=part(k, True, 1, 1), dst_ref=part(k, False, near_row, 1),
            send_sem=x_send.at[k], recv_sem=x_recv.at[k],
            device_id=(partner, gy), device_id_type=MESH)

    def z_copy(k):
        return pltpu.make_async_remote_copy(
            src_ref=part(k, False, near_row, 1), dst_ref=part(k, False, far_row, 1),
            send_sem=z_send.at[k], recv_sem=z_recv.at[k],
            device_id=(relay_to, gy), device_id_type=MESH)

    def y_copy(k, kind, up):
        row = (1, near_row, far_row)[kind]
        return pltpu.make_async_remote_copy(
            src_ref=part(k, kind == 0, row, 1), dst_ref=part(k, False, row, 0 if up else 2),
            send_sem=y_send.at[kind, 1 if up else 0, k], recv_sem=y_recv.at[kind, 1 if up else 0, k],
            device_id=(gx, gy + 1 if up else gy - 1), device_id_type=MESH)

    def y_arrival(k, kind, up):
        row = (1, near_row, far_row)[kind]
        return pltpu.make_async_remote_copy(
            src_ref=part(k, kind == 0, row, 1), dst_ref=part(k, False, row, 0 if up else 2),
            send_sem=y_send.at[kind, 1 if up else 0, k], recv_sem=y_recv.at[kind, 1 if up else 0, k],
            device_id=(gx, gy - 1 if up else gy + 1), device_id_type=MESH)

    barrier = pltpu.get_barrier_semaphore()

    def greet(target, there):
        @pl.when(there)
        def _():
            pl.semaphore_signal(barrier, inc=1, device_id=target, device_id_type=MESH)

    pl.semaphore_signal(barrier, inc=1, device_id=(partner, gy), device_id_type=MESH)
    greet((relay_to, gy), has_to)
    greet((relay_from, gy), has_from)
    greet((gx, gy + 1), has_up)
    greet((gx, gy - 1), has_down)
    total = 1
    for there in (has_to, has_from, has_up, has_down):
        total = total + jnp.where(there, 1, 0)
    pl.semaphore_wait(barrier, total)

    def y_starts(k, kind):
        @pl.when(has_up)
        def _():
            y_copy(k, kind, True).start()

        @pl.when(has_down)
        def _():
            y_copy(k, kind, False).start()

    for k in range(2):
        x_copy(k).start()
        y_starts(k, 0)
    def relay(k):
        x_arrival(k).wait_recv()

        @pl.when(has_to)
        def _():
            z_copy(k).start()

        y_starts(k, 1)

    def spread(k):
        @pl.when(has_from)
        def _():
            z_copy(k).wait_recv()
            y_starts(k, 2)

    def own_block(block, _):
        prepare_own(block, geo_ref, gx, gy, *own)
        lanes = pl.ds(pl.multiple_of(block * BLOCK, BLOCK), BLOCK)
        feats[4 * blocks + block] = features(geo_ref[:, lanes], gx, gy, False).astype(jnp.bfloat16)
        return 0

    lax.fori_loop(0, blocks, own_block, 0)
    for k in range(2):
        relay(k)
    for k in range(2, items):
        x_copy(k).start()
    for k in range(2):
        spread(k)
    for k in range(2, items):
        y_starts(k, 0)

    def near_blocks(slot):
        def near_block(block, _):
            lanes = pl.ds(pl.multiple_of(block * BLOCK, BLOCK), BLOCK)
            feats[slot * blocks + block] = features(geos[slot, :, lanes], gx, gy, False).astype(jnp.bfloat16)
            return 0

        lax.fori_loop(0, blocks, near_block, 0)

    near_blocks(near_row * 3 + 1)

    @pl.when(has_from)
    def _():
        near_blocks(far_row * 3 + 1)

    def y_gets(kind, up):
        gets = has_down if up else has_up
        return gets & has_from if kind == 2 else gets

    for kind in range(3):
        for up in (True, False):
            @pl.when(y_gets(kind, up))
            def _():
                y_arrival(1, kind, up).wait_recv()
                near_blocks((1, near_row, far_row)[kind] * 3 + (0 if up else 2))

    def slot_ids(s):
        return list_ref[0, s], list_ref[1, s]

    piece = BLOCK // 4

    def out_copies(which, tile, s):
        return [pltpu.make_async_copy(tile.at[pl.ds(c * piece, piece)], tiles.at[s, pl.ds(c * piece, piece)],
                                      out_sems.at[which, c]) for c in range(4)]

    a0, b0 = slot_ids(0)
    for c in range(BLOCK // PART):
        align_part(c, a0, b0, own, feats, work0)

    events = {}
    for c, at in enumerate((0, 2, 4, 7)):
        events.setdefault(at * rounds // 16, []).append((relay, c + 2))
    for c, at in enumerate((2, 4, 7, 9)):
        events.setdefault(at * rounds // 16, []).append((spread, c + 2))
    held = tile0, tile1, tile2, tile3

    def round_step(i, _):
        for at, calls in events.items():
            @pl.when(i == at)
            def _():
                for call, k in calls:
                    call(k)

        for which, tile in enumerate(held):
            now, later = (work0, work1) if which % 2 == 0 else (work1, work0)
            s = 4 * i + which
            a_next, b_next = slot_ids(jnp.minimum(s + 1, 4 * rounds - 1))

            @pl.when(i > 0)
            def _():
                for copy in out_copies(which, tile, s):
                    copy.wait()

            align_part(0, a_next, b_next, own, feats, later)
            tile_part(0, now, tile)
            for copy in out_copies(which, tile, s):
                copy.start()
        return 0

    lax.fori_loop(0, rounds, round_step, 0)
    for which, tile in enumerate(held):
        for copy in out_copies(which, tile, 4 * rounds - 4 + which):
            copy.wait()

    for k in range(items):
        x_copy(k).wait_send()

        @pl.when(has_to)
        def _():
            z_copy(k).wait_send()

        for kind in range(3):
            for up, sends, gets in ((True, has_up, has_down), (False, has_down, has_up)):
                if kind == 2:
                    sends = sends & has_from
                    gets = gets & has_from

                @pl.when(sends)
                def _():
                    y_copy(k, kind, up).wait_send()

                if k != 1:
                    @pl.when(gets)
                    def _():
                        y_arrival(k, kind, up).wait_recv()


def product_kernel(nx, ny, list_ref, lists, geo_ref, feats_ref, pan_ref, pans, tiles,
                   out_ref, count_of, todo, slot_of, own_along, own_coarse, own_fine, feats, pan_all,
                   aligned0, aligned1, square0, square1, tile0, tile1, product, stored, sems, stored_sems, feat_sem):
    own = own_along, own_coarse, own_fine
    work0, work1 = (aligned0, square0), (aligned1, square1)
    gx = lax.axis_index("gx")
    gy = lax.axis_index("gy")
    fil, width = pan_ref.shape
    blocks = fil // BLOCK
    near = 9 * blocks
    spare = blocks * near
    sides = [(sx, sy) for sx in range(3) for sy in range(3)]

    def present(slot):
        sx, sy = sides[slot]
        there = (gx + (sx - 1) >= 0) & (gx + (sx - 1) < nx)
        return there & (gy + (sy - 1) >= 0) & (gy + (sy - 1) < ny)

    def load(slot, block):
        source = pan_ref.at[pl.ds(block * BLOCK, BLOCK)] if slot == 4 else pans.at[slot, pl.ds(block * BLOCK, BLOCK)]
        return pltpu.make_async_copy(source, pan_all.at[slot * blocks + block], sems.at[slot, block])

    feat_load = pltpu.make_async_copy(feats_ref, feats, feat_sem)
    for slot in (4, 0, 1, 2, 3, 5, 6, 7, 8):
        for block in range(blocks):
            load(slot, block).start()
    feat_load.start()

    def clear(i, _):
        count_of[i] = 0
        return 0

    lax.fori_loop(0, spare + 8, clear, 0, unroll=8)

    def add(a, b, wanted, n):
        where_ = jnp.where(wanted, a * near + b, spare)
        seen = count_of[where_]
        todo[n] = where_
        count_of[where_] = seen + 1
        return n + jnp.where(wanted & (seen == 0), 1, 0)

    def own_pair(s, n):
        slot_of[n] = s
        return add(list_ref[0, s], list_ref[1, s], True, n)

    ready = lax.fori_loop(0, list_ref[2, 0], own_pair, 0)
    depth = stored.shape[0]

    def fetch(i):
        slot = lax.rem(i, depth)
        return pltpu.make_async_copy(tiles.at[slot_of[i]], stored.at[slot], stored_sems.at[slot])

    for i in range(depth):
        @pl.when(i < ready)
        def _():
            fetch(i).start()

    def mirrored(s, n):
        q = list_ref[1, s] - 4 * blocks
        a = list_ref[0, s]
        return add(q, 4 * blocks + a, (q >= 0) & (q < blocks) & (q != a), n)

    n = lax.fori_loop(0, list_ref[2, 0], mirrored, ready)
    for slot in range(9):
        if slot != 4:
            def their_pair(s, n, slot=slot):
                q = lists[slot, 1, s] - (8 - slot) * blocks
                return add(q, slot * blocks + lists[slot, 0, s], (q >= 0) & (q < blocks), n)

            total = jnp.where(present(slot), lists[slot, 2, 0], 0)
            n = lax.fori_loop(0, total, their_pair, n)

    def own_block(block, _):
        prepare_own(block, geo_ref, gx, gy, *own)
        return 0

    lax.fori_loop(0, blocks, own_block, 0)
    out_ref[...] = jnp.zeros_like(out_ref)
    for slot in range(9):
        for block in range(blocks):
            load(slot, block).wait()

    def entry(i):
        inside = i < n
        index = jnp.where(inside, todo[jnp.where(inside, i, 0)], 4 * blocks)
        a = index // near
        return a, index - a * near, jnp.where(inside, count_of[index], 0).astype(jnp.float32)

    def product_part(c, a, b, times, tile):
        first = pl.multiple_of(a * BLOCK + c * PART, PART)
        here = jnp.dot(tile[pl.ds(c * PART, PART), :], pan_all[b], preferred_element_type=jnp.float32)
        out_ref[pl.ds(first, PART), :] += times * here

    def ready_item(i, _):
        a, b, times = entry(i)
        fetch(i).wait()
        for c in range(BLOCK // PART):
            product_part(c, a, b, times, stored.at[lax.rem(i, depth)])

        @pl.when(i + depth < ready)
        def _():
            fetch(i + depth).start()

        return 0

    lax.fori_loop(0, ready, ready_item, 0)
    feat_load.wait()

    @pl.when(n > ready)
    def _():
        a0, b0, _ = entry(ready)
        for c in range(BLOCK // PART):
            align_part(c, a0, b0, own, feats, work0)
        tile1[...] = jnp.zeros_like(tile1)

        def two_items(j, before):
            i = ready + 2 * j
            for half, now, later, tile, past in (
                (0, work0, work1, tile0, tile1), (1, work1, work0, tile1, tile0)):
                a, b, times = entry(i + half)
                a_next, b_next, _ = entry(i + half + 1)
                for c in range(BLOCK // PART):
                    align_part(c, a_next, b_next, own, feats, later)
                sum_a, sum_b, sum_times = before
                product[...] = jnp.dot(past[...], pan_all[sum_b], preferred_element_type=jnp.float32)
                for c in range(BLOCK // PART):
                    tile_part(c, now, tile)
                out_ref[pl.ds(pl.multiple_of(sum_a * BLOCK, BLOCK), BLOCK), :] += sum_times * product[...]
                before = (a, b, times)
            return before

        last = lax.fori_loop(0, (n - ready + 1) // 2, two_items, (jnp.int32(0), jnp.int32(4 * blocks), jnp.float32(0)))
        for c in range(BLOCK // PART):
            product_part(c, *last, tile1)


def shards(nx, ny, geometry, panel, pair_first, pair_second, pair_count):
    fil, width = panel.shape
    blocks = fil // BLOCK
    near = 9 * blocks
    pair_len = pair_first.shape[0]
    long = -(-pair_len // 128) * 128
    made = 4 * (-(-pair_len // 4))
    table = jnp.pad(jnp.stack([pair_first, pair_second, jnp.broadcast_to(pair_count, (pair_len,))]),
                    ((0, 5), (0, long - pair_len)))
    items = CHUNKS + 2
    anywhere = pl.BlockSpec(memory_space=pl.ANY)
    vmem = pl.BlockSpec(memory_space=pltpu.VMEM)
    smem = pl.BlockSpec(memory_space=pltpu.SMEM)
    square = (BLOCK, BLOCK)
    lists, pans, tiles, feats = pl.pallas_call(
        functools.partial(halo_kernel, nx, ny),
        out_shape=(
            jax.ShapeDtypeStruct((9, 8, long), jnp.int32),
            jax.ShapeDtypeStruct((9, fil, width), jnp.bfloat16),
            jax.ShapeDtypeStruct((made,) + square, jnp.bfloat16),
            jax.ShapeDtypeStruct((near, 128, BLOCK), jnp.bfloat16),
        ),
        in_specs=[anywhere, smem, vmem, anywhere],
        out_specs=(anywhere, anywhere, anywhere, vmem),
        scratch_shapes=[
            pltpu.VMEM((9, 8, fil), jnp.float32),
            pltpu.VMEM((blocks, BLOCK, 32), jnp.bfloat16),
            pltpu.VMEM((blocks, BLOCK, 16), jnp.bfloat16),
            pltpu.VMEM((blocks, BLOCK, 80), jnp.bfloat16),
            pltpu.VMEM(square, jnp.float32),
            pltpu.VMEM(square, jnp.float32),
            pltpu.VMEM(square, jnp.float32),
            pltpu.VMEM(square, jnp.float32),
            pltpu.VMEM(square, jnp.bfloat16),
            pltpu.VMEM(square, jnp.bfloat16),
            pltpu.VMEM(square, jnp.bfloat16),
            pltpu.VMEM(square, jnp.bfloat16),
            pltpu.SemaphoreType.DMA((items,)),
            pltpu.SemaphoreType.DMA((items,)),
            pltpu.SemaphoreType.DMA((items,)),
            pltpu.SemaphoreType.DMA((items,)),
            pltpu.SemaphoreType.DMA((3, 2, items)),
            pltpu.SemaphoreType.DMA((3, 2, items)),
            pltpu.SemaphoreType.DMA((4, 4)),
        ],
        compiler_params=pltpu.CompilerParams(
            collective_id=0, has_side_effects=True, vmem_limit_bytes=VMEM_LIMIT),
        name="halo",
    )(table, table, geometry, panel)

    depth = 4
    return pl.pallas_call(
        functools.partial(product_kernel, nx, ny),
        out_shape=jax.ShapeDtypeStruct((fil, width), jnp.float32),
        in_specs=[smem, smem, vmem, anywhere, anywhere, anywhere, anywhere],
        out_specs=vmem,
        scratch_shapes=[
            pltpu.SMEM((blocks * near + 8,), jnp.int32),
            pltpu.SMEM((blocks * near + 8,), jnp.int32),
            pltpu.SMEM((blocks * near + 8,), jnp.int32),
            pltpu.VMEM((blocks, BLOCK, 32), jnp.bfloat16),
            pltpu.VMEM((blocks, BLOCK, 16), jnp.bfloat16),
            pltpu.VMEM((blocks, BLOCK, 80), jnp.bfloat16),
            pltpu.VMEM((near, 128, BLOCK), jnp.bfloat16),
            pltpu.VMEM((near, BLOCK, width), jnp.bfloat16),
            pltpu.VMEM(square, jnp.float32),
            pltpu.VMEM(square, jnp.float32),
            pltpu.VMEM(square, jnp.float32),
            pltpu.VMEM(square, jnp.float32),
            pltpu.VMEM(square, jnp.bfloat16),
            pltpu.VMEM(square, jnp.bfloat16),
            pltpu.VMEM((BLOCK, width), jnp.float32),
            pltpu.VMEM((depth,) + square, jnp.bfloat16),
            pltpu.SemaphoreType.DMA((9, blocks)),
            pltpu.SemaphoreType.DMA((depth,)),
            pltpu.SemaphoreType.DMA,
        ],
        compiler_params=pltpu.CompilerParams(vmem_limit_bytes=VMEM_LIMIT),
        name="products",
    )(table, lists, geometry, feats, panel, pans, tiles)


def solution(mesh):
    nx, ny = mesh.shape["gx"], mesh.shape["gy"]
    in_specs = (
        P(None, ("gx", "gy")),
        P(("gx", "gy"), None),
        P(("gx", "gy")),
        P(("gx", "gy")),
        P(("gx", "gy")),
    )
    out_specs = P(("gx", "gy"), None)
    return jax.shard_map(functools.partial(shards, nx, ny), mesh=mesh, in_specs=in_specs,
                         out_specs=out_specs, check_vma=False)
```

profile of v0, /device:TPU:10, one launch (start us, length us, event | category | flops | bytes accessed | tf_op | source)
XLA Modules:
  0.0 110.1 jit_solution(16160613278986227929)
XLA Ops:
  0.7 0.1 pad.7.clone
  0.7 0.7 add_add_fusion
  1.5 0.6 pad.4.table_ref.list_ref
  2.1 66.2 %halo.1 = (s32[9,8,128]{2,1,0:T(8,128)}, bf16[9,4096,128]{2,1,0:T(8,128)(2,1)}, bf16[64,512,512]{2,1,0:T(8,128)(2,1)}, bf16[72,128,512]{2,1,0:T(8,128)(2,1)}) custom-call(s32[8,128]{1,0:T(8,128)} %pad.4.table_ref.list_ref, s32[8,128]{1,0:T(8,128)} %pad.4.table_ref.list_ref, f32[8,4096]{1,0:T(8,128)} %geo_ref.3, bf16[4096,128]{1,0:T(8,128)(2,1)} %pan_ref.3), custom_call_target="tpu_custom_call" | custom-call | tf_op jit(solution)/shard_map/halo/pallas_call | solution.py:454
  68.2 41.9 %products.1 = f32[4096,128]{1,0:T(8,128)} custom-call(s32[8,128]{1,0:T(8,128)} %pad.4.table_ref.list_ref, s32[9,8,128]{2,1,0:T(8,128)} %get-tuple-element.9.lists, f32[8,4096]{1,0:T(8,128)} %geo_ref.3, bf16[72,128,512]{2,1,0:T(8,128)(2,1)} %get-tuple-element.10.feats_ref, bf16[4096,128]{1,0:T(8,128)(2,1)} %pan_ref.3, ...), custom_call_target="tpu_custom_call" | custom-call | tf_op jit(solution)/shard_map/products/pallas_call | solution.py:491
where the time goes:
time: 112 us; the launch traced here: 110 us
  Pallas kernels  108 us (96%)
    pallas_call x1, Pallas kernels, shards(): pl.pallas_call(functools.partial(halo_kernel, nx, ny), out_shape=(jax.Sha...  66.2 us
    pallas_call x1, Pallas kernels, shards(): pl.pallas_call(functools.partial(product_kernel, nx, ny), out_shape=jax.S...  41.9 us

commit v1 on v0

--- a/solution.py
+++ b/solution.py
@@ -244,10 +244,10 @@
         align_part(c, a0, b0, own, feats, work0)
 
     events = {}
-    for c, at in enumerate((0, 2, 4, 7)):
-        events.setdefault(at * rounds // 16, []).append((relay, c + 2))
-    for c, at in enumerate((2, 4, 7, 9)):
-        events.setdefault(at * rounds // 16, []).append((spread, c + 2))
+    for c, at in enumerate((0, 1, 3, 5)):
+        events.setdefault(at * rounds // 12, []).append((relay, c + 2))
+    for c, at in enumerate((2, 4, 6, 8)):
+        events.setdefault(at * rounds // 12, []).append((spread, c + 2))
     held = tile0, tile1, tile2, tile3
 
     def round_step(i, _):
@@ -346,7 +346,8 @@
         slot_of[n] = s
         return add(list_ref[0, s], list_ref[1, s], True, n)
 
-    ready = lax.fori_loop(0, list_ref[2, 0], own_pair, 0)
+    made = jnp.minimum(list_ref[2, 0], tiles.shape[0])
+    ready = lax.fori_loop(0, made, own_pair, 0)
     depth = stored.shape[0]
 
     def fetch(i):
@@ -363,7 +364,11 @@
         a = list_ref[0, s]
         return add(q, 4 * blocks + a, (q >= 0) & (q < blocks) & (q != a), n)
 
-    n = lax.fori_loop(0, list_ref[2, 0], mirrored, ready)
+    def late_pair(s, n):
+        return add(list_ref[0, s], list_ref[1, s], True, n)
+
+    n = lax.fori_loop(made, list_ref[2, 0], late_pair, ready)
+    n = lax.fori_loop(0, list_ref[2, 0], mirrored, n)
     for slot in range(9):
         if slot != 4:
             def their_pair(s, n, slot=slot):
@@ -443,7 +448,7 @@
     near = 9 * blocks
     pair_len = pair_first.shape[0]
     long = -(-pair_len // 128) * 128
-    made = 4 * (-(-pair_len // 4))
+    made = 4 * (-(-3 * pair_len // 16))
     table = jnp.pad(jnp.stack([pair_first, pair_second, jnp.broadcast_to(pair_count, (pair_len,))]),
                     ((0, 5), (0, long - pair_len)))
     items = CHUNKS + 2

time: 112 us -> 108 us (0.964)
  the two profiles are of different devices: /device:TPU:10 before, /device:TPU:17 now
where the time goes in v1:
time: 108 us; the launch traced here: 109 us
  Pallas kernels  107 us (99%)
    pallas_call x1, Pallas kernels, shards(): pl.pallas_call(functools.partial(halo_kernel, nx, ny), out_shape=(jax.Sha...  56.4 us
    pallas_call x1, Pallas kernels, shards(): pl.pallas_call(functools.partial(product_kernel, nx, ny), out_shape=jax.S...  50.4 us

profile of v1, /device:TPU:17, one launch (start us, length us, event | category | flops | bytes accessed | tf_op | source)
XLA Modules:
  0.0 108.8 jit_solution(287326556737394480)
XLA Ops:
  0.7 0.1 pad.7.clone
  0.7 0.7 add_add_fusion
  1.5 0.6 pad.4.table_ref.list_ref
  2.1 56.4 %halo.1 = (s32[9,8,128]{2,1,0:T(8,128)}, bf16[9,4096,128]{2,1,0:T(8,128)(2,1)}, bf16[48,512,512]{2,1,0:T(8,128)(2,1)}, bf16[72,128,512]{2,1,0:T(8,128)(2,1)}) custom-call(s32[8,128]{1,0:T(8,128)} %pad.4.table_ref.list_ref, s32[8,128]{1,0:T(8,128)} %pad.4.table_ref.list_ref, f32[8,4096]{1,0:T(8,128)} %geo_ref.3, bf16[4096,128]{1,0:T(8,128)(2,1)} %pan_ref.3), custom_call_target="tpu_custom_call" | custom-call | tf_op jit(solution)/shard_map/halo/pallas_call | solution.py:459
  58.4 50.4 %products.1 = f32[4096,128]{1,0:T(8,128)} custom-call(s32[8,128]{1,0:T(8,128)} %pad.4.table_ref.list_ref, s32[9,8,128]{2,1,0:T(8,128)} %get-tuple-element.9.lists, f32[8,4096]{1,0:T(8,128)} %geo_ref.3, bf16[72,128,512]{2,1,0:T(8,128)(2,1)} %get-tuple-element.10.feats_ref, bf16[4096,128]{1,0:T(8,128)(2,1)} %pan_ref.3, ...), custom_call_target="tpu_custom_call" | custom-call | tf_op jit(solution)/shard_map/products/pallas_call | solution.py:496
